TPU v7x, 32 devices: a whole 2x2x4 slice. The times are simulated.
32 devices in a mesh: node: 8 (over z, x), sector: 4 (over y, core).
Axes of the slice: x: 2, y: 2, z: 4, core: 2. Of those that a mesh axis runs over, the one named last changes fastest.
Arguments:
- returns: bfloat16 [1024, 12, 2048], P('node'), may hold values from -0.29882812 to 0.29882812
- barrier_scale: float32 [1024, 12], P('node'), may hold values from 0.25 to 4
- parent_ids: int32 [1024, 1], P('node'), may hold values from 0 to 7; in each aligned block of 128 rows (0 to 127, 128 to 255, ...) at most 32 rows name the same one
- loadings: float32 [8, 2048], P('node'), may hold values from -3 to 3
- own_variance: float32 [8, 2048], P('node'), may hold values from 0.5 to 4
- sector_sizes: int32 [64], replicated, may hold values from 1 to 64, 2048 in all
Outputs:
- cholesky_rows: float32 [8, 2048, 2048], P('node', 'sector')
Inputs may be any that keep to these rules, and one draw needn't show every extreme that they name: `parent_ids`: of the 128 children held by one index of node (aligned blocks of rows), at most 32 share a parent; in every draw some block has exactly 32 children of one parent. `sector_sizes`: the sizes sum to 2048, and the largest is 64.
All inputs are finite; a program needn't handle non-finite values.
Results may differ from a plain program's by a relative error of at most 0.00045.
Values may be sent and summed in bfloat16 or wider, within the bound.
No kernel may reach another device: no remote copies, remote signals or barrier semaphores. Data moves between devices by JAX's collectives and lax.ppermute only.
A program may use at most 192 MiB of HBM per device.

v0:
```python
import jax
import jax.numpy as jnp
from jax import lax
from jax.sharding import PartitionSpec as P


def broadcast(array, axis, root):
    mine = lax.axis_index(axis) == root
    return lax.psum(jnp.where(mine, array, jnp.zeros_like(array)), axis)


def sector_labels(sector_sizes, count):
    sector_ends = jnp.cumsum(sector_sizes)
    asset_index = jnp.arange(count, dtype=jnp.int32)
    return jnp.sum((asset_index[:, None] >= sector_ends[None, :]).astype(jnp.int32), axis=1)


def on_device(returns, barrier_scale, parent_ids, loadings, own_variance, sector_sizes):
    node_count = lax.axis_size("node")
    sector_count = lax.axis_size("sector")
    my_index = lax.axis_index("sector")
    child_count, row_count, asset_count = returns.shape
    capacity = max(2, 2 * child_count // node_count)
    band_rows = asset_count // sector_count
    first_row = my_index * band_rows
    scaled = (jnp.sqrt(barrier_scale)[:, :, None] * returns.astype(jnp.float32)).astype(
        jnp.bfloat16
    )
    targets = parent_ids[:, 0]
    child_index = jnp.arange(child_count, dtype=jnp.int32)
    earlier = (targets[:, None] == targets[None, :]) & (child_index[None, :] < child_index[:, None])
    position = jnp.sum(earlier.astype(jnp.int32), axis=1)
    slot_of = targets * capacity + position
    slot_index = jnp.arange(node_count * capacity, dtype=jnp.int32)
    onehot = (slot_of[None, :] == slot_index[:, None]).astype(jnp.bfloat16)
    share_rows = row_count // sector_count
    my_share = lax.dynamic_slice_in_dim(scaled, my_index * share_rows, share_rows, 1)
    flattened = my_share.reshape(child_count, share_rows * asset_count)
    outbox = jnp.dot(onehot, flattened, preferred_element_type=jnp.float32).astype(jnp.bfloat16)
    outbox = outbox.reshape(node_count, capacity, share_rows, asset_count)
    arrived = lax.all_to_all(outbox, "node", split_axis=0, concat_axis=0, tiled=True)
    inbox = lax.all_gather(arrived, "sector", axis=2, tiled=True)
    rows_all = inbox.reshape(-1, asset_count)
    my_columns = lax.dynamic_slice_in_dim(rows_all, first_row, band_rows, 1)
    schur = lax.dot_general(
        my_columns, rows_all, (((0,), (0,)), ((), ())), preferred_element_type=jnp.float32
    )
    sector_of = sector_labels(sector_sizes, asset_count)
    row_labels = lax.dynamic_slice_in_dim(sector_of, first_row, band_rows)
    loading = loadings[0]
    row_loading = lax.dynamic_slice_in_dim(loading, first_row, band_rows)
    row_variance = lax.dynamic_slice_in_dim(own_variance[0], first_row, band_rows)
    asset_index = jnp.arange(asset_count, dtype=jnp.int32)
    on_diagonal = (
        asset_index[None, :] == (first_row + jnp.arange(band_rows, dtype=jnp.int32))[:, None]
    )
    covariance = jnp.where(
        row_labels[:, None] == sector_of[None, :],
        row_loading[:, None] * loading[None, :],
        jnp.zeros((), jnp.float32),
    )
    normal_matrix = (
        schur
        + covariance
        + jnp.where(on_diagonal, row_variance[:, None], jnp.zeros((), jnp.float32))
    )
    blocks = []
    for step_index in range(sector_count):
        offset = step_index * band_rows
        column_block = normal_matrix[:, offset : offset + band_rows]
        is_root = my_index == step_index
        if offset > 0:
            left_part = jnp.concatenate(blocks, axis=1)
            reduced = column_block - jnp.dot(
                left_part,
                left_part.T,
                precision=lax.Precision.HIGHEST,
                preferred_element_type=jnp.float32,
            )
        else:
            reduced = column_block
        guarded = jnp.where(is_root, reduced, jnp.eye(band_rows, dtype=jnp.float32))
        diag_factor = jnp.linalg.cholesky(guarded)
        if step_index + 1 < sector_count:
            if offset > 0:
                root_panel = jnp.concatenate([left_part, diag_factor], axis=1)
            else:
                root_panel = diag_factor
            arrived_panel = broadcast(root_panel, "sector", step_index)
            root_diag = arrived_panel[:, offset:]
            if offset > 0:
                residual_block = column_block - jnp.dot(
                    left_part,
                    arrived_panel[:, :offset].T,
                    precision=lax.Precision.HIGHEST,
                    preferred_element_type=jnp.float32,
                )
            else:
                residual_block = column_block
            below_diag = jax.scipy.linalg.solve_triangular(
                root_diag, residual_block.T, lower=True
            ).T
            new_block = jnp.where(
                my_index > step_index,
                below_diag,
                jnp.where(is_root, root_diag, jnp.zeros((), jnp.float32)),
            )
        else:
            new_block = jnp.where(is_root, diag_factor, jnp.zeros((), jnp.float32))
        blocks.append(new_block)
    cholesky_rows = jnp.concatenate(blocks, axis=1)
    return cholesky_rows[None]


def solution(mesh):
    in_specs = (
        P("node", None, None),
        P("node", None),
        P("node", None),
        P("node", None),
        P("node", None),
        P(),
    )
    out_specs = P("node", "sector", None)
    return jax.shard_map(
        on_device, mesh=mesh, in_specs=in_specs, out_specs=out_specs, check_vma=False
    )
```

profile of v0, /device:TPU:1, one launch (start us, length us, event | category | flops | bytes accessed | tf_op | source)
XLA Modules:
  0.0 974.1 jit_solution(15884194691169355756)
XLA Ops:
  21.0 76.0 %all_to_all.5 = bf16[8,32,3,2048]{3,1,2,0:T(8,128)(2,1)S(1)} all-to-all(bf16[8,32,3,2048]{3,1,2,0:T(8,128)(2,1)S(1)} %copy.115), channel_id=1, replica_groups=mesh['node'=8,'sector'=4] {'node'}, dimensions={0} | all-to-all | bytes 6291456 | tf_op jit(solution)/shard_map/all_to_all | solution.py:41
  101.0 81.0 %all-gather.2.cloned.1.call-done = bf16[8,32,12,2048]{3,1,0,2:T(8,128)(2,1)} async-done(((bf16[8,32,3,2048]{3,1,0,2:T(8,128)(2,1)}), bf16[8,32,12,2048]{3,1,0,2:T(8,128)(2,1)}) %all-gather.2.cloned.1.call-update) | async-done | bytes 12582928 | tf_op jit(solution)/shard_map/all_gather | solution.py:42
  182.1 14.1 %copy.117 = bf16[8,32,12,2048]{3,2,1,0:T(8,128)(2,1)} copy(bf16[8,32,12,2048]{3,1,0,2:T(8,128)(2,1)} %all-gather.2.cloned.1.call-done) | data formatting | bytes 25165824 | tf_op jit(solution)/shard_map/all_gather | solution.py:42
  196.1 19.9 %reshape.88 = bf16[3072,2048]{1,0:T(8,128)(2,1)} reshape(bf16[8,32,12,2048]{3,2,1,0:T(8,128)(2,1)} %copy.117) | data formatting | bytes 25165824 | tf_op jit(solution)/shard_map/reshape | solution.py:43
  216.1 11.6 %select_add_fusion = f32[512,2048]{0,1:T(8,128)S(1)} fusion(bf16[3072,2048]{1,0:T(8,128)(2,1)} %reshape.88, s32[]{:T(128)S(6)} %select_n.105, f32[512]{0:T(512)S(1)} %bitcast.197, s32[512]{0:T(512)S(1)} %iota_add_fusion, f32[2048]{0:T(1024)S(1)} %bitcast.200, f32[512]{0:T(512)S(1)} %bitcast.198, s32[512]{0:T(512)S(1)} %dynamic_slice.17, ...), kind=kOutput, calls=%fused_computation.8 | convolution fusion | flops 6449790976 | bytes 19947524 | tf_op jit(solution)/shard_map/dot_general | solution.py:45
  231.2 11.7 %cholesky.462 = f32[128,128]{1,0:T(8,128)S(1)} custom-call(f32[128,128]{1,0:T(8,128)S(1)} %cholesky.746), custom_call_target="Cholesky" | custom-call | tf_op jit(solution)/shard_map/jit(cholesky)/cholesky | solution.py:83
  255.3 11.7 %cholesky.481 = f32[128,128]{1,0:T(8,128)S(1)} custom-call(f32[128,128]{1,0:T(8,128)S(1)} %cholesky.750), custom_call_target="Cholesky" | custom-call | tf_op jit(solution)/shard_map/jit(cholesky)/cholesky | solution.py:83
  267.4 10.2 %custom-call.35 = f32[1,128,128]{1,2,0:T(8,128)S(1)} custom-call(f32[1,128,128]{2,1,0:T(8,128)S(1)} %get-tuple-element.131), custom_call_target="InvertDiagBlocksLowerTriangular" | custom-call | tf_op jit(solution)/shard_map/jit(cholesky)/cholesky | solution.py:83
  279.7 11.7 %cholesky.502 = f32[128,128]{1,0:T(8,128)S(1)} custom-call(f32[128,128]{1,0:T(8,128)S(1)} %cholesky.755), custom_call_target="Cholesky" | custom-call | tf_op jit(solution)/shard_map/jit(cholesky)/cholesky | solution.py:83
  303.0 11.8 %cholesky.519 = f32[128,128]{1,0:T(8,128)S(1)} custom-call(f32[128,128]{1,0:T(8,128)S(1)} %convolution_subtract_fusion.22), custom_call_target="Cholesky" | custom-call | tf_op jit(solution)/shard_map/jit(cholesky)/cholesky | solution.py:83
  321.5 35.6 %all-reduce.5.cloned.1.call-done = f32[512,512]{0,1:T(8,128)} async-done(((f32[512,512]{0,1:T(8,128)}), f32[512,512]{0,1:T(8,128)}) %all-reduce.5.cloned.1.call-update) | async-done | bytes 1048592 | tf_op jit(solution)/shard_map/psum | solution.py:9
  359.5 11.9 %while.6 = (s32[]{:T(128)}, f32[512,512]{0,1:T(8,128)}, s32[4,2]{0,1:T(2,128)S(1)}, f32[4,128,128]{2,1,0:T(8,128)S(1)}, s32[]{:T(128)}) while((s32[]{:T(128)}, f32[512,512]{0,1:T(8,128)}, s32[4,2]{0,1:T(2,128)S(1)}, f32[4,128,128]{2,1,0:T(8,128)S(1)}, s32[]{:T(128)}) %tuple.79), condition=%wide.while_cond, body=%wide.while_body.sunk | while | flops 2 | bytes 393321 | solution.py:100
  371.4 39.3 %custom-call.37 = f32[4,128,128]{1,2,0:T(8,128)S(1)} custom-call(f32[4,128,128]{2,1,0:T(8,128)S(1)} %get-tuple-element.27), custom_call_target="InvertDiagBlocksLowerTriangular" | custom-call | tf_op jit(solution)/shard_map/jit(_solve_triangular)/triangular_solve | solution.py:100
  421.6 11.7 %cholesky.534 = f32[128,128]{1,0:T(8,128)S(1)} custom-call(f32[128,128]{1,0:T(8,128)S(1)} %cholesky.759), custom_call_target="Cholesky" | custom-call | tf_op jit(solution)/shard_map/jit(cholesky)/cholesky | solution.py:83
  446.4 11.7 %cholesky.553 = f32[128,128]{1,0:T(8,128)S(1)} custom-call(f32[128,128]{1,0:T(8,128)S(1)} %cholesky.763), custom_call_target="Cholesky" | custom-call | tf_op jit(solution)/shard_map/jit(cholesky)/cholesky | solution.py:83
  469.9 11.7 %cholesky.574 = f32[128,128]{1,0:T(8,128)S(1)} custom-call(f32[128,128]{1,0:T(8,128)S(1)} %cholesky.768), custom_call_target="Cholesky" | custom-call | tf_op jit(solution)/shard_map/jit(cholesky)/cholesky | solution.py:83
  481.8 10.2 %custom-call.40 = f32[1,128,128]{1,2,0:T(8,128)S(1)} custom-call(f32[1,128,128]{2,1,0:T(8,128)S(1)} %get-tuple-element.123), custom_call_target="InvertDiagBlocksLowerTriangular" | custom-call | tf_op jit(solution)/shard_map/jit(cholesky)/cholesky | solution.py:83
  493.6 11.7 %cholesky.591 = f32[128,128]{1,0:T(8,128)S(1)} custom-call(f32[128,128]{1,0:T(8,128)S(1)} %convolution_subtract_fusion.21), custom_call_target="Cholesky" | custom-call | tf_op jit(solution)/shard_map/jit(cholesky)/cholesky | solution.py:83
  512.4 52.0 %all-reduce.7.cloned.1.call-done = f32[512,1024]{0,1:T(8,128)} async-done(((f32[512,1024]{0,1:T(8,128)}), f32[512,1024]{0,1:T(8,128)}) %all-reduce.7.cloned.1.call-update) | async-done | bytes 2097168 | tf_op jit(solution)/shard_map/psum | solution.py:9
  566.9 11.5 %while.7 = (s32[]{:T(128)}, f32[512,512]{0,1:T(8,128)}, s32[4,2]{0,1:T(2,128)S(1)}, f32[4,128,128]{2,1,0:T(8,128)S(1)}, s32[]{:T(128)}) while((s32[]{:T(128)}, f32[512,512]{0,1:T(8,128)}, s32[4,2]{0,1:T(2,128)S(1)}, f32[4,128,128]{2,1,0:T(8,128)S(1)}, s32[]{:T(128)}) %tuple.96), condition=%wide.while_cond.clone, body=%wide.while_body.clone.sunk | while | flops 2 | bytes 393321 | solution.py:100
  579.1 40.3 %custom-call.41 = f32[4,128,128]{1,2,0:T(8,128)S(1)} custom-call(f32[4,128,128]{2,1,0:T(8,128)} %copy-done.9), custom_call_target="InvertDiagBlocksLowerTriangular" | custom-call | tf_op jit(solution)/shard_map/jit(_solve_triangular)/triangular_solve | solution.py:100
  637.5 12.1 %cholesky.606 = f32[128,128]{1,0:T(8,128)S(1)} custom-call(f32[128,128]{1,0:T(8,128)S(1)} %cholesky.772), custom_call_target="Cholesky" | custom-call | tf_op jit(solution)/shard_map/jit(cholesky)/cholesky | solution.py:83
  662.5 11.7 %cholesky.625 = f32[128,128]{1,0:T(8,128)S(1)} custom-call(f32[128,128]{1,0:T(8,128)S(1)} %cholesky.776), custom_call_target="Cholesky" | custom-call | tf_op jit(solution)/shard_map/jit(cholesky)/cholesky | solution.py:83
  686.0 11.9 %cholesky.646 = f32[128,128]{1,0:T(8,128)S(1)} custom-call(f32[128,128]{1,0:T(8,128)S(1)} %cholesky.781), custom_call_target="Cholesky" | custom-call | tf_op jit(solution)/shard_map/jit(cholesky)/cholesky | solution.py:83
  709.5 11.7 %cholesky.663 = f32[128,128]{1,0:T(8,128)S(1)} custom-call(f32[128,128]{1,0:T(8,128)S(1)} %convolution_subtract_fusion.20), custom_call_target="Cholesky" | custom-call | tf_op jit(solution)/shard_map/jit(cholesky)/cholesky | solution.py:83
  728.8 68.6 %all-reduce.9.cloned.1.call-done = f32[512,1536]{0,1:T(8,128)} async-done(((f32[512,1536]{0,1:T(8,128)}), f32[512,1536]{0,1:T(8,128)}) %all-reduce.9.cloned.1.call-update) | async-done | bytes 3145744 | tf_op jit(solution)/shard_map/psum | solution.py:9
  807.5 40.5 %custom-call.45 = f32[4,128,128]{1,2,0:T(8,128)S(1)} custom-call(f32[4,128,128]{2,1,0:T(8,128)} %copy-done.10), custom_call_target="InvertDiagBlocksLowerTriangular" | custom-call | tf_op jit(solution)/shard_map/jit(_solve_triangular)/triangular_solve | solution.py:100
  869.5 11.7 %cholesky.678 = f32[128,128]{1,0:T(8,128)S(1)} custom-call(f32[128,128]{1,0:T(8,128)S(1)} %cholesky.785), custom_call_target="Cholesky" | custom-call | tf_op jit(solution)/shard_map/jit(cholesky)/cholesky | solution.py:83
  894.1 11.7 %cholesky.697 = f32[128,128]{1,0:T(8,128)S(1)} custom-call(f32[128,128]{1,0:T(8,128)S(1)} %cholesky.789), custom_call_target="Cholesky" | custom-call | tf_op jit(solution)/shard_map/jit(cholesky)/cholesky | solution.py:83
  906.0 10.0 %custom-call.47 = f32[1,128,128]{1,2,0:T(8,128)S(1)} custom-call(f32[1,128,128]{2,1,0:T(8,128)S(1)} %get-tuple-element.113), custom_call_target="InvertDiagBlocksLowerTriangular" | custom-call | tf_op jit(solution)/shard_map/jit(cholesky)/cholesky | solution.py:83
  917.8 11.7 %cholesky.718 = f32[128,128]{1,0:T(8,128)S(1)} custom-call(f32[128,128]{1,0:T(8,128)S(1)} %cholesky.794), custom_call_target="Cholesky" | custom-call | tf_op jit(solution)/shard_map/jit(cholesky)/cholesky | solution.py:83
  941.1 11.7 %cholesky.735 = f32[128,128]{1,0:T(8,128)S(1)} custom-call(f32[128,128]{1,0:T(8,128)S(1)} %convolution_subtract_fusion.19), custom_call_target="Cholesky" | custom-call | tf_op jit(solution)/shard_map/jit(cholesky)/cholesky | solution.py:83
  (282 shorter events, 259.4 us)
Async XLA Ops:
  6.5 175.5 %all-gather.2.cloned.1.call-start = ((), (), s32[]{:S(2)}) async-start(), calls=%async_computation.1 | async-start | bytes 15728640 | tf_op jit(solution)/shard_map/all_gather | solution.py:42
  6.5 2.5 copy-start.11
  6.5 2.5 copy-start.14
  99.1 0.7 copy-start.12
  99.1 1.2 copy-start.13
  99.2 257.9 %all-reduce.5.cloned.1.call-start = ((), (), s32[]{:S(2)}) async-start(), calls=%async_computation.2 | async-start | bytes 2097152 | tf_op jit(solution)/shard_map/psum | solution.py:9
  227.7 2.0 copy-start.3
  230.2 1.0 copy-start.6
  321.4 243.0 %all-reduce.7.cloned.1.call-start = ((), (), s32[]{:S(2)}) async-start(), calls=%async_computation.3 | async-start | bytes 4194304 | tf_op jit(solution)/shard_map/psum | solution.py:9
  371.4 45.3 %copy-start.2 = (f32[512,512]{0,1:T(8,128)S(1)}, f32[512,512]{0,1:T(8,128)}, u32[]{:S(2)}) copy-start(f32[512,512]{0,1:T(8,128)} %all-reduce.5.cloned.1.call-done) | copy-start | bytes 3145732
  420.6 1.0 copy-start.7
  512.3 285.1 %all-reduce.9.cloned.1.call-start = ((), (), s32[]{:S(2)}) async-start(), calls=%async_computation.4 | async-start | bytes 6291456 | tf_op jit(solution)/shard_map/psum | solution.py:9
  564.4 55.1 %copy-start = (f32[512,1024]{0,1:T(8,128)S(1)}, f32[512,1024]{0,1:T(8,128)}, u32[]{:S(2)}) copy-start(f32[512,1024]{0,1:T(8,128)} %all-reduce.7.cloned.1.call-done) | copy-start | bytes 6291460
  578.4 0.7 copy-start.9
  622.6 6.2 copy-start.1
  636.5 1.0 copy-start.8
  806.7 0.7 copy-start.10
  858.2 1.0 copy-start.4
  868.6 1.0 copy-start.5
Sparse Core Ops, SparseCore 0:
  99.3 82.7 all-gather.1
  321.5 35.5 all-reduce.4
  512.5 51.8 all-reduce.6
  728.9 68.4 all-reduce.8
where the time goes:
time: 985 us; the launch traced here: 974 us
  other arithmetic  460 us (47%)
  waiting for transfers between devices  237 us (24%)
  local copies, waits for them, and re-layouts  101 us (10%)
  blocking collectives  76 us (8%)
  matrix products  75.3 us (8%)
  between operations  24.8 us (3%)
    another operation x60, other arithmetic, on_device(): diag_factor = jnp.linalg.cholesky(guarded)  318 us
    psum x3, waiting for transfers between devices, broadcast(): return lax.psum(jnp.where(mine, array, jnp.zeros_like(array)), axis)  156 us
    another operation x7, other arithmetic, on_device(): jax.scipy.linalg.solve_triangular(root_diag, residual_block.T, lower=True)  126 us
    all_gather x1, waiting for transfers between devices, on_device(): inbox = lax.all_gather(arrived, 'sector', axis=2, tiled=True)  81 us
    all_to_all x1, blocking collectives, on_device(): lax.all_to_all(outbox, 'node', split_axis=0, concat_axis=0, tiled=True)  76 us
    another operation x64, local copies, waits for them, and re-layouts, on_device(): jax.scipy.linalg.solve_triangular(root_diag, residual_block.T, lower=True)  31 us
    another operation x24, matrix products, on_device(): diag_factor = jnp.linalg.cholesky(guarded)  24.7 us
    reshape x1, local copies, waits for them, and re-layouts, on_device(): rows_all = inbox.reshape(-1, asset_count)  19.9 us
  transfers between devices with their start and end apart: 4, of which 4 were waited for; matrix products, arithmetic and copies ran while one was open for 0% of the time, Pallas kernels for 0%

commit v1 on v0

v1 whole, which is shorter than its diff:
```python
import functools
import jax
import jax.numpy as jnp
from jax import lax
from jax.experimental import pallas as pl
from jax.experimental.pallas import tpu as pltpu
from jax.sharding import PartitionSpec as P

F32 = jnp.float32
BF16 = jnp.bfloat16
LANES = 128
BLOCK = 128
HALF = 64
VMEM_LIMIT = 56 * 2**20


def split(x):
    high = x.astype(BF16)
    return high, (x - high.astype(F32)).astype(BF16)


def dot3(a, b, dims):
    one = lambda x, y: lax.dot_general(x, y, (dims, ((), ())), preferred_element_type=F32)
    (ah, al), (bh, bl) = a, b
    return one(ah, bh) + (one(ah, bl) + one(al, bh))


NT = ((1,), (1,))
TN = ((0,), (0,))
NN = ((1,), (0,))


def sweep_rows(rows_in, first, comb, rout):
    n = rows_in[0].shape[1]
    lane = lax.broadcasted_iota(jnp.int32, (8, n), 1)
    sub = lax.broadcasted_iota(jnp.int32, (8, n), 0)
    rows = list(rows_in)
    of_row = lambda v, i: jnp.broadcast_to(v[i : i + 1, :], (8, n))
    of_lane = lambda v, j: jnp.take_along_axis(v, jnp.full((8, n), j, jnp.int32), axis=1)
    for g in range(len(rows)):
        o = first + 8 * g
        cur = rows[g]
        cols = [of_lane(cur, o + j) for j in range(8)]
        in_group = (lane >= o) & (lane < o + 8)
        raw = cur
        aug = jnp.where(in_group, jnp.where(lane == o + sub, 1.0, 0.0), cur)
        w_rows = r_rows = None
        for x in range(0, 8, 2):
            y = x + 1
            a, b, c = of_row(cols[x], x), of_row(cols[y], x), of_row(cols[y], y)
            inv_det = pltpu.reciprocal(a * c - b * b, approx=True)
            cx = jnp.where(sub == x, -1.0, jnp.where(sub == y, 0.0, cols[x]))
            cy = jnp.where(sub == y, -1.0, jnp.where(sub == x, 0.0, cols[y]))
            mx, my = inv_det * (c * cx - b * cy), inv_det * (a * cy - b * cx)
            pair = (sub == x) | (sub == y)
            for l in range(y + 1, 8):
                cols[l] = jnp.where(pair, 0.0, cols[l]) - (
                    mx * of_row(cols[l], x) + my * of_row(cols[l], y)
                )
            ra = lax.rsqrt(a)
            bra = b * ra
            rc = lax.rsqrt(c - bra * bra)
            scale = jnp.where(sub == x, ra, rc)
            back = jnp.where(sub == x, 0.0, bra) * ra
            ax, ay, rx, ry = of_row(aug, x), of_row(aug, y), of_row(raw, x), of_row(raw, y)
            wn = (aug - back * ax) * scale
            rn = (raw - back * rx) * scale
            w_rows = wn if w_rows is None else jnp.where(sub >= x, wn, w_rows)
            r_rows = rn if r_rows is None else jnp.where(sub >= x, rn, r_rows)
            aug = jnp.where(pair, 0.0, aug) - (mx * ax + my * ay)
            raw = raw - (mx * rx + my * ry)
        comb[o : o + 8, :] = w_rows
        rout[o : o + 8, :] = jnp.where(lane >= o, r_rows, 0.0)
        solved = [of_row(aug, j) for j in range(8)]
        for h in range(g + 1, len(rows)):
            acc = [None, None]
            for j in range(8):
                t = of_lane(rows[h], o + j) * solved[j]
                acc[j % 2] = t if acc[j % 2] is None else acc[j % 2] + t
            rows[h] = jnp.where(in_group, 0.0, rows[h]) - (acc[0] + acc[1])


def factor_block(rest, comb, rout):
    n = BLOCK
    sweep_rows([rest[8 * h : 8 * h + 8, :] for h in range(HALF // 8)], 0, comb, rout)
    row = lax.broadcasted_iota(jnp.int32, (HALF, n), 0)
    lane = lax.broadcasted_iota(jnp.int32, (HALF, n), 1)
    top = jnp.where((lane < HALF) & (lane > row), 0.0, comb[0:HALF, :])
    low = jnp.where(lane < HALF, 0.0, rest[HALF:n, :])
    th, tl = split(top)
    low = low - dot3((th[:, HALF:], tl[:, HALF:]), (th, tl), TN)
    sweep_rows([low[8 * h : 8 * h + 8, :] for h in range(HALF // 8)], HALF, comb, rout)
    row = lax.broadcasted_iota(jnp.int32, (n, n), 0)
    lane = lax.broadcasted_iota(jnp.int32, (n, n), 1)
    return jnp.where(lane <= row, comb[...], 0.0)


def band_kernel(off, width, prior, *refs):
    count = len(prior)
    it = iter(refs)
    take = lambda k: [next(it) for _ in range(k)]
    (label_row, load_row, label_col, load_col, var_col) = take(5)
    x_hbm = take(count + 1)
    lh_hbm, ll_hbm = take(max(count - 1, 0)), take(max(count - 1, 0))
    ih_hbm, il_hbm = take(count), take(count)
    lfull, lh_out, ll_out, ih_out, il_out = take(5)
    x_mine, x_other, lh, ll, ih, il, mat, ph, pl_, diag, comb, rout, sems = take(13)

    def copy(src, dst, k):
        return pltpu.make_async_copy(src, dst, sems.at[k])

    mine = copy(x_hbm[count], x_mine, 0)
    mine.start()
    others = [copy(x_hbm[j], x_other.at[j], 1 + j) for j in range(count)]
    for c in others:
        c.start()
    later = []
    for j in range(count):
        o, w = prior[j]
        if j > 0:
            later.append(copy(lh_hbm[j - 1], lh.at[pl.ds(o, w), pl.ds(0, o)], 1 + count + 4 * j))
            later.append(copy(ll_hbm[j - 1], ll.at[pl.ds(o, w), pl.ds(0, o)], 2 + count + 4 * j))
        later.append(copy(ih_hbm[j], ih.at[j], 3 + count + 4 * j))
        later.append(copy(il_hbm[j], il.at[j], 4 + count + 4 * j))
    for c in later:
        c.start()
    mine.wait()

    def normal_part(x, o, w):
        gram = lax.dot_general(x_mine[...], x, (NT, ((), ())), preferred_element_type=F32)
        same = label_col[...] == label_row[:, o : o + w]
        return gram + jnp.where(same, load_col[...] * load_row[:, o : o + w], 0.0)

    for j in range(count):
        o, w = prior[j]
        others[j].wait()
        mat[:, o : o + w] = normal_part(x_other[j], o, w)
    on_diag = lax.broadcasted_iota(jnp.int32, (width, width), 0) == lax.broadcasted_iota(
        jnp.int32, (width, width), 1
    )
    diag[...] = normal_part(x_mine[...], off, width) + jnp.where(on_diag, var_col[...], 0.0)
    for c in later:
        c.wait()
    for j in range(count):
        o, w = prior[j]
        acc = mat[:, o : o + w]
        if j > 0:
            acc = acc - dot3(
                (ph[:, :o], pl_[:, :o]), (lh[o : o + w, :o], ll[o : o + w, :o]), NT
            )
        part = dot3(split(acc), (ih[j], il[j]), NT)
        lfull[:, o : o + w] = part
        ph[:, o : o + w], pl_[:, o : o + w] = split(part)
    if count:
        lh_out[...] = ph[...]
        ll_out[...] = pl_[...]
        diag[...] = diag[...] - dot3((ph[...], pl_[...]), (ph[...], pl_[...]), NT)
    lfull[:, off : off + width] = jnp.zeros((width, width), F32)
    rest = lfull.shape[1] - off - width
    if rest:
        lfull[:, off + width :] = jnp.zeros((width, rest), F32)
    ih_out[...] = jnp.zeros((width, width), BF16)
    il_out[...] = jnp.zeros((width, width), BF16)

    row = lax.broadcasted_iota(jnp.int32, (width, BLOCK), 0)

    def step(k, carry):
        at = pl.multiple_of(k * BLOCK, BLOCK)
        here = pl.ds(at, BLOCK)
        w = factor_block(diag[here, here], comb, rout)
        wh, wl = split(w)
        column = dot3(split(diag[:, here]), (wh, wl), NT)
        column = jnp.where(row >= at + BLOCK, column, 0.0)
        ch, cl = split(column)
        diag[...] = diag[...] - dot3((ch, cl), (ch, cl), NT)
        out_at = pl.ds(pl.multiple_of(off + at, BLOCK), BLOCK)
        lfull[:, out_at] = column
        lfull[here, out_at] = jnp.transpose(rout[...])
        lh_k, ll_k = split(lfull[here, off : off + width])
        cols = lax.broadcasted_iota(jnp.int32, (BLOCK, width), 1)
        lh_k = jnp.where(cols < at, lh_k, jnp.zeros_like(lh_k))
        ll_k = jnp.where(cols < at, ll_k, jnp.zeros_like(ll_k))
        below = -dot3((lh_k, ll_k), (ih_out[...], il_out[...]), NN)
        rows = dot3((wh, wl), split(below), NN)
        ih_out[here, :], il_out[here, :] = split(rows)
        ih_out[here, here], il_out[here, here] = wh, wl
        return carry

    lax.fori_loop(0, width // BLOCK, step, 0)


def band(off, width, total, prior, vectors, xs, lhs, lls, ihs, ils):
    count = len(prior)
    depth = xs[0].shape[1]
    label_row, load_row, label_col, load_col, var_col = vectors
    any_spec = pl.BlockSpec(memory_space=pl.ANY)
    vm = pl.BlockSpec(memory_space=pltpu.VMEM)
    rows_of = lambda v: v[off : off + width]
    args = [label_row, load_row, rows_of(label_col), rows_of(load_col), rows_of(var_col)]
    in_specs = [vm] * 5
    big = list(xs) + list(lhs[1:]) + list(lls[1:]) + list(ihs) + list(ils)
    args += big
    in_specs += [any_spec] * len(big)
    left = max(off, BLOCK)
    slots = max(count, 1)
    widest = max([w for _, w in prior] + [BLOCK])
    return pl.pallas_call(
        functools.partial(band_kernel, off, width, prior),
        out_shape=[
            jax.ShapeDtypeStruct((width, total), F32),
            jax.ShapeDtypeStruct((width, left), BF16),
            jax.ShapeDtypeStruct((width, left), BF16),
            jax.ShapeDtypeStruct((width, width), BF16),
            jax.ShapeDtypeStruct((width, width), BF16),
        ],
        in_specs=in_specs,
        out_specs=[vm] * 5,
        scratch_shapes=[
            pltpu.VMEM((width, depth), BF16),
            pltpu.VMEM((slots, widest, depth), BF16),
            pltpu.VMEM((left, left), BF16),
            pltpu.VMEM((left, left), BF16),
            pltpu.VMEM((slots, widest, widest), BF16),
            pltpu.VMEM((slots, widest, widest), BF16),
            pltpu.VMEM((width, left), F32),
            pltpu.VMEM((width, left), BF16),
            pltpu.VMEM((width, left), BF16),
            pltpu.VMEM((width, width), F32),
            pltpu.VMEM((BLOCK, BLOCK), F32),
            pltpu.VMEM((BLOCK, BLOCK), F32),
            pltpu.SemaphoreType.DMA((8 + 5 * slots,)),
        ],
        compiler_params=pltpu.CompilerParams(vmem_limit_bytes=VMEM_LIMIT),
        name="band_%d" % off,
    )(*args)


def gather_kernel(rows_per, capacity, info, slots, returns, scale, out, stage):
    dests = out.shape[0]

    def one(d, carry):
        for s in range(capacity):
            child = slots[d * capacity + s]
            keep = jnp.where(child >= 0, 1.0, 0.0).astype(F32)
            at = jnp.maximum(child, 0)
            value = returns[at].astype(F32) * (scale[at] * keep)
            stage[s * rows_per : (s + 1) * rows_per, :] = value
        out[d] = jnp.transpose(stage[...]).astype(BF16)
        return carry

    lax.fori_loop(0, dests, one, 0)


def gather(returns, scale, slots, column_block, dests, capacity):
    children, rows_per, _ = returns.shape
    depth = capacity * rows_per
    grid_spec = pltpu.PrefetchScalarGridSpec(
        num_scalar_prefetch=2,
        grid=(1,),
        in_specs=[
            pl.BlockSpec((children, rows_per, LANES), lambda i, info, slots: (0, 0, info[0])),
            pl.BlockSpec((children, rows_per, LANES), lambda i, info, slots: (0, 0, 0)),
        ],
        out_specs=pl.BlockSpec((dests, LANES, depth), lambda i, info, slots: (0, 0, 0)),
        scratch_shapes=[pltpu.VMEM((depth, LANES), F32)],
    )
    return pl.pallas_call(
        functools.partial(gather_kernel, rows_per, capacity),
        out_shape=jax.ShapeDtypeStruct((dests, LANES, depth), BF16),
        grid_spec=grid_spec,
        compiler_params=pltpu.CompilerParams(vmem_limit_bytes=VMEM_LIMIT),
        name="gather",
    )(column_block, slots, returns, scale)


def on_device(returns, barrier_scale, parent_ids, loadings, own_variance, sector_sizes):
    node_count = lax.axis_size("node")
    sector_count = lax.axis_size("sector")
    my_index = lax.axis_index("sector")
    child_count, row_count, asset_count = returns.shape
    capacity = max(2, 2 * child_count // node_count)
    band_rows = asset_count // sector_count
    targets = parent_ids[:, 0]
    child_index = jnp.arange(child_count, dtype=jnp.int32)
    earlier = (targets[:, None] == targets[None, :]) & (child_index[None, :] < child_index[:, None])
    position = jnp.sum(earlier.astype(jnp.int32), axis=1)
    slot_of = targets * capacity + position
    slot_index = jnp.arange(node_count * capacity, dtype=jnp.int32)
    slots = jnp.max(
        jnp.where(slot_of[None, :] == slot_index[:, None], child_index[None, :], -1), axis=1
    )
    scale = jnp.broadcast_to(jnp.sqrt(barrier_scale)[:, :, None], (child_count, row_count, LANES))

    sector_ends = jnp.cumsum(sector_sizes)
    asset_index = jnp.arange(asset_count, dtype=jnp.int32)
    labels = jnp.sum((asset_index[:, None] >= sector_ends[None, :]).astype(jnp.int32), axis=1)
    vectors = (
        labels[None, :],
        loadings,
        labels[:, None],
        loadings[0][:, None],
        own_variance[0][:, None],
    )

    width = sector_count * LANES
    prior, xs, lhs, lls, ihs, ils, bands = [], [], [], [], [], [], []
    for off in range(0, asset_count, width):
        block = (off // LANES + my_index)[None].astype(jnp.int32)
        outbox = gather(returns, scale, slots, block, node_count, capacity)
        arrived = lax.all_to_all(outbox, "node", split_axis=0, concat_axis=0, tiled=True)
        inbox = lax.all_gather(arrived, "sector", axis=0)
        x = inbox.transpose(0, 2, 1, 3).reshape(width, -1)
        xs.append(x)
        full, lh, ll, ih, il = band(
            off, width, asset_count, tuple(prior), vectors, xs, lhs, lls, ihs, ils
        )
        prior.append((off, width))
        bands.append(full)
        lhs.append(lh)
        lls.append(ll)
        ihs.append(ih)
        ils.append(il)
    rows = jnp.concatenate(bands, axis=0)
    return lax.dynamic_slice_in_dim(rows, my_index * band_rows, band_rows, 0)[None]


def solution(mesh):
    in_specs = (
        P("node", None, None),
        P("node", None),
        P("node", None),
        P("node", None),
        P("node", None),
        P(),
    )
    out_specs = P("node", "sector", None)
    return jax.shard_map(
        on_device, mesh=mesh, in_specs=in_specs, out_specs=out_specs, check_vma=False
    )
```

time: 985 us -> 318 us (0.32)
  other arithmetic: 460 us -> 9.38 us
  waiting for transfers between devices: 237 us -> 6.22 us
  Pallas kernels: 0 us -> 142 us
  matrix products: 75.3 us -> 0 us
  local copies, waits for them, and re-layouts: 101 us -> 46.2 us
  blocking collectives: 76 us -> 95.8 us
  between operations: 24.8 us -> 13.8 us
    another operation x69 -> x2, other arithmetic: 445 us -> 0.2 us  [the longest x60 318 us: on_device(): diag_factor = jnp.linalg.cholesky(guarded)]
    psum x3 -> x0, waiting for transfers between devices: 156 us -> none  [broadcast(): return lax.psum(jnp.where(mine, array, jnp.zeros_like(array)), axis)]
    pallas_call x0 -> x8, Pallas kernels: none -> 142 us  [the longest x4 123 us: band(): pl.pallas_call(functools.partial(band_kernel, off, width, prior), out_sha...]
    all_gather x1 -> x4, waiting for transfers between devices: 81 us -> 6.15 us  [on_device(): inbox = lax.all_gather(arrived, 'sector', axis=0)]
    another operation x45 -> x0, matrix products: 39.9 us -> none  [the longest x24 24.7 us: on_device(): diag_factor = jnp.linalg.cholesky(guarded)]
    dot_general x7 -> x0, matrix products: 35.4 us -> none  [the longest x3 14.3 us: on_device(): jnp.dot(left_part, left_part.T, precision=lax.Precision.HIGHEST, preferre...]
    another operation x111 -> x1, local copies, waits for them, and re-layouts: 33.3 us -> 0.1 us  [the longest x64 31 us: on_device(): jax.scipy.linalg.solve_triangular(root_diag, residual_block.T, lower=True)]
    reshape x3 -> x0, local copies, waits for them, and re-layouts: 30.4 us -> none  [the longest x1 19.9 us: on_device(): rows_all = inbox.reshape(-1, asset_count)]
  transfers between devices with their start and end apart: 4 -> 4, of which waited for: 4 -> 1; matrix products, arithmetic and copies ran while one was open for 0% -> 9% of each run, Pallas kernels for 0% -> 4%
where the time goes in v1:
time: 318 us; the launch traced here: 313 us
  Pallas kernels  142 us (45%)
  blocking collectives  95.8 us (30%)
  local copies, waits for them, and re-layouts  46.2 us (15%)
  between operations  13.8 us (4%)
  other arithmetic  9.38 us (3%)
  waiting for transfers between devices  6.22 us (2%)
    pallas_call x4, Pallas kernels, band(): pl.pallas_call(functools.partial(band_kernel, off, width, prior), out_sha...  123 us
    all_to_all x4, blocking collectives, on_device(): lax.all_to_all(outbox, 'node', split_axis=0, concat_axis=0, tiled=True)  95.8 us
    unnamed x17, local copies, waits for them, and re-layouts  19.3 us
    pallas_call x4, Pallas kernels, gather(): pl.pallas_call(functools.partial(gather_kernel, rows_per, capacity), out_...  18.2 us
    all_gather x4, local copies, waits for them, and re-layouts, on_device(): inbox = lax.all_gather(arrived, 'sector', axis=0)  15.1 us
    slice x15, local copies, waits for them, and re-layouts, band(): rows_of = lambda v: v[off:off + width]  10.4 us
    broadcast_in_dim x1, other arithmetic, on_device(): lax.dynamic_slice_in_dim(rows, my_index * band_rows, band_rows, 0)[None]  6.82 us
  transfers between devices with their start and end apart: 4, of which 1 were waited for; matrix products, arithmetic and copies ran while one was open for 9% of the time, Pallas kernels for 4%

profile of v1, /device:TPU:1, one launch (start us, length us, event | category | flops | bytes accessed | tf_op | source)
XLA Modules:
  0.0 313.2 jit_solution(12430459049620357142)
XLA Ops:
  6.5 0.9 convert_reduce_fusion.1
  8.8 9.7 %copy.63.returns = bf16[128,12,2048]{2,1,0:T(8,128)(2,1)} copy(bf16[128,12,2048]{2,0,1:T(8,128)(2,1)} %param.6) | data formatting | bytes 12582912 | tf_op args[0]
  18.6 1.3 broadcast_in_dim.48.scale
  19.9 4.5 %gather.4 = bf16[8,128,384]{2,1,0:T(8,128)(2,1)} custom-call(s32[1]{0:T(128)} %bitcast.5.info, s32[256]{0:T(256)} %select_reduce_fusion.slots, bf16[128,12,2048]{2,1,0:T(8,128)(2,1)} %copy.63.returns, f32[128,12,128]{2,1,0:T(8,128)} %broadcast_in_dim.48.scale), custom_call_target="tpu_custom_call" | custom-call | tf_op jit(solution)/shard_map/gather/pallas_call | solution.py:267
  24.4 25.8 %all_to_all.20 = bf16[8,128,384]{2,1,0:T(8,128)(2,1)} all-to-all(bf16[8,128,384]{2,1,0:T(8,128)(2,1)} %gather.4), channel_id=1, replica_groups=mesh['node'=8,'sector'=4] {'node'}, dimensions={0} | all-to-all | bytes 1572864 | tf_op jit(solution)/shard_map/all_to_all | solution.py:310
  50.3 4.5 %gather.5 = bf16[8,128,384]{2,1,0:T(8,128)(2,1)} custom-call(s32[1]{0:T(128)} %bitcast.12.info, s32[256]{0:T(256)} %select_reduce_fusion.slots, bf16[128,12,2048]{2,1,0:T(8,128)(2,1)} %copy.63.returns, f32[128,12,128]{2,1,0:T(8,128)} %broadcast_in_dim.48.scale), custom_call_target="tpu_custom_call" | custom-call | tf_op jit(solution)/shard_map/gather/pallas_call | solution.py:267
  54.8 23.3 %all_to_all.21 = bf16[8,128,384]{2,1,0:T(8,128)(2,1)} all-to-all(bf16[8,128,384]{2,1,0:T(8,128)(2,1)} %gather.5), channel_id=1, replica_groups=mesh['node'=8,'sector'=4] {'node'}, dimensions={0} | all-to-all | bytes 1572864 | tf_op jit(solution)/shard_map/all_to_all | solution.py:310
  78.2 4.5 %gather.6 = bf16[8,128,384]{2,1,0:T(8,128)(2,1)} custom-call(s32[1]{0:T(128)} %bitcast.18.info, s32[256]{0:T(256)} %select_reduce_fusion.slots, bf16[128,12,2048]{2,1,0:T(8,128)(2,1)} %copy.63.returns, f32[128,12,128]{2,1,0:T(8,128)} %broadcast_in_dim.48.scale), custom_call_target="tpu_custom_call" | custom-call | tf_op jit(solution)/shard_map/gather/pallas_call | solution.py:267
  82.7 23.4 %all_to_all.22 = bf16[8,128,384]{2,1,0:T(8,128)(2,1)} all-to-all(bf16[8,128,384]{2,1,0:T(8,128)(2,1)} %gather.6), channel_id=1, replica_groups=mesh['node'=8,'sector'=4] {'node'}, dimensions={0} | all-to-all | bytes 1572864 | tf_op jit(solution)/shard_map/all_to_all | solution.py:310
  106.2 4.7 %gather.7 = bf16[8,128,384]{2,1,0:T(8,128)(2,1)} custom-call(s32[1]{0:T(128)} %bitcast.24.info, s32[256]{0:T(256)} %select_reduce_fusion.slots, bf16[128,12,2048]{2,1,0:T(8,128)(2,1)} %copy.63.returns, f32[128,12,128]{2,1,0:T(8,128)} %broadcast_in_dim.48.scale), custom_call_target="tpu_custom_call" | custom-call | tf_op jit(solution)/shard_map/gather/pallas_call | solution.py:267
  110.8 23.4 %all_to_all.23 = bf16[8,128,384]{2,1,0:T(8,128)(2,1)} all-to-all(bf16[8,128,384]{2,1,0:T(8,128)(2,1)} %gather.7), channel_id=1, replica_groups=mesh['node'=8,'sector'=4] {'node'}, dimensions={0} | all-to-all | bytes 1572864 | tf_op jit(solution)/shard_map/all_to_all | solution.py:310
  134.7 0.9 copy.65.refs_2_
  135.6 0.9 copy.66.refs_3_
  139.0 0.9 copy.72.refs_4_
  139.9 0.9 copy.75.refs_2_
  140.8 0.9 copy.76.refs_3_
  142.5 0.9 copy.80.refs_2_
  143.4 0.9 copy.81.refs_3_
  145.1 3.8 %copy.64 = bf16[4,8,128,384]{3,1,2,0:T(8,128)(2,1)S(1)} copy(bf16[4,8,128,384]{3,2,1,0:T(8,128)(2,1)} %bitcast.64) | data formatting | bytes 6291456 | tf_op jit(solution)/shard_map/all_gather | solution.py:311
  148.8 2.4 copy.83
  151.2 3.8 %copy.69 = bf16[4,8,128,384]{3,1,2,0:T(8,128)(2,1)S(1)} copy(bf16[4,8,128,384]{3,2,1,0:T(8,128)(2,1)} %bitcast.65) | data formatting | bytes 6291456 | tf_op jit(solution)/shard_map/all_gather | solution.py:311
  155.0 2.4 copy.84
  157.4 3.8 %copy.74 = bf16[4,8,128,384]{3,1,2,0:T(8,128)(2,1)S(1)} copy(bf16[4,8,128,384]{3,2,1,0:T(8,128)(2,1)} %bitcast.66) | data formatting | bytes 6291456 | tf_op jit(solution)/shard_map/all_gather | solution.py:311
  161.2 2.4 copy.85
  163.6 6.1 %all-gather.15.cloned.1.call-done = bf16[32,128,384]{2,1,0:T(8,128)(2,1)} async-done(((bf16[8,128,384]{2,1,0:T(8,128)(2,1)}), bf16[32,128,384]{2,1,0:T(8,128)(2,1)}) %all-gather.15.cloned.1.call-update) | async-done | bytes 3145744 | tf_op jit(solution)/shard_map/all_gather | solution.py:311
  169.7 3.8 %copy.79 = bf16[4,8,128,384]{3,1,2,0:T(8,128)(2,1)S(1)} copy(bf16[4,8,128,384]{3,2,1,0:T(8,128)(2,1)} %bitcast.67) | data formatting | bytes 6291456 | tf_op jit(solution)/shard_map/all_gather | solution.py:311
  173.5 2.4 copy.86
  175.9 23.9 %band_0.1 = (f32[512,2048]{1,0:T(8,128)}, bf16[512,128]{1,0:T(8,128)(2,1)}, bf16[512,128]{1,0:T(8,128)(2,1)}, bf16[512,512]{1,0:T(8,128)(2,1)}, bf16[512,512]{1,0:T(8,128)(2,1)}) custom-call(s32[1,2048]{1,0:T(1,128)} %bitcast.68, f32[1,2048]{1,0:T(1,128)} %refs_1_.7, s32[512,1]{1,0:T(8,128)} %copy.65.refs_2_, f32[512,1]{1,0:T(8,128)} %copy.66.refs_3_, ...), custom_call_target="tpu_custom_call" | custom-call | tf_op jit(solution)/shard_map/band_0/pallas_call | solution.py:207
  199.8 28.2 %band_512.1 = (f32[512,2048]{1,0:T(8,128)}, bf16[512,512]{1,0:T(8,128)(2,1)}, bf16[512,512]{1,0:T(8,128)(2,1)}, bf16[512,512]{1,0:T(8,128)(2,1)}, bf16[512,512]{1,0:T(8,128)(2,1)}) custom-call(s32[1,2048]{1,0:T(1,128)} %bitcast.69, f32[1,2048]{1,0:T(1,128)} %refs_1_.7, s32[512,1]{1,0:T(8,128)} %copy.70.refs_2_, f32[512,1]{1,0:T(8,128)} %copy.71.refs_3_, ...), custom_call_target="tpu_custom_call" | custom-call | tf_op jit(solution)/shard_map/band_512/pallas_call | solution.py:207
  228.0 32.7 %band_1024.1 = (f32[512,2048]{1,0:T(8,128)}, bf16[512,1024]{1,0:T(8,128)(2,1)}, bf16[512,1024]{1,0:T(8,128)(2,1)}, bf16[512,512]{1,0:T(8,128)(2,1)}, bf16[512,512]{1,0:T(8,128)(2,1)}) custom-call(s32[1,2048]{1,0:T(1,128)} %bitcast.70, f32[1,2048]{1,0:T(1,128)} %refs_1_.7, s32[512,1]{1,0:T(8,128)} %copy.75.refs_2_, f32[512,1]{1,0:T(8,128)} %copy.76.refs_3_, ...), custom_call_target="tpu_custom_call" | custom-call | tf_op jit(solution)/shard_map/band_1024/pallas_call | solution.py:207
  260.8 38.6 %band_1536.1 = (f32[512,2048]{1,0:T(8,128)}, bf16[512,1536]{1,0:T(8,128)(2,1)}, bf16[512,1536]{1,0:T(8,128)(2,1)}, bf16[512,512]{1,0:T(8,128)(2,1)}, bf16[512,512]{1,0:T(8,128)(2,1)}) custom-call(s32[1,2048]{1,0:T(1,128)} %bitcast.71, f32[1,2048]{1,0:T(1,128)} %refs_1_.7, s32[512,1]{1,0:T(8,128)} %copy.80.refs_2_, f32[512,1]{1,0:T(8,128)} %copy.81.refs_3_, ...), custom_call_target="tpu_custom_call" | custom-call | tf_op jit(solution)/shard_map/band_1536/pallas_call | solution.py:207
  299.4 6.8 %fusion.3 = f32[1,512,2048]{2,1,0:T(8,128)} fusion(s32[]{:T(128)S(6)} %select_n.8, f32[512,2048]{1,0:T(8,128)S(1)} %copy-done, f32[512,2048]{1,0:T(8,128)} %get-tuple-element.22, f32[512,2048]{1,0:T(8,128)} %get-tuple-element.27, f32[512,2048]{1,0:T(8,128)} %get-tuple-element.32), kind=kLoop, calls=%fused_computation.7 | loop fusion | flops 3145728 | bytes 20971524 | tf_op jit(solution)/shard_map/broadcast_in_dim | solution.py:324
  (39 shorter events, 6.4 us)
Async XLA Ops:
  6.5 138.5 %all-gather.9.cloned.1.call-start = ((), (), s32[]{:S(2)}) async-start(), calls=%async_computation.4 | async-start | bytes 3932160 | tf_op jit(solution)/shard_map/all_gather | solution.py:311
  8.8 9.7 %copy-start.3 = (f32[128,12]{0,1:T(8,128)S(1)}, f32[128,12]{0,1:T(8,128)}, u32[]{:S(2)}) copy-start(f32[128,12]{0,1:T(8,128)} %param.7) | copy-start | bytes 18436
  50.2 101.0 %all-gather.11.cloned.1.call-start = ((), (), s32[]{:S(2)}) async-start(), calls=%async_computation.5 | async-start | bytes 3932160 | tf_op jit(solution)/shard_map/all_gather | solution.py:311
  78.1 79.3 %all-gather.13.cloned.1.call-start = ((), (), s32[]{:S(2)}) async-start(), calls=%async_computation.6 | async-start | bytes 3932160 | tf_op jit(solution)/shard_map/all_gather | solution.py:311
  106.1 63.7 %all-gather.15.cloned.1.call-start = ((), (), s32[]{:S(2)}) async-start(), calls=%async_computation.7 | async-start | bytes 3932160 | tf_op jit(solution)/shard_map/all_gather | solution.py:311
  106.1 28.1 %copy-start.5 = (s32[64]{0:T(128)S(1)}, s32[64]{0:T(128)}, u32[]{:S(2)}) copy-start(s32[64]{0:T(128)} %param.11) | copy-start | bytes 772
  106.1 29.4 %copy-start.2 = (f32[1,2048]{1,0:T(1,128)S(1)}, f32[1,2048]{1,0:T(1,128)}, u32[]{:S(2)}) copy-start(f32[1,2048]{1,0:T(1,128)} %refs_1_.7) | copy-start | bytes 24580
  106.1 30.3 %copy-start.4 = (f32[1,2048]{1,0:T(1,128)S(1)}, f32[1,2048]{1,0:T(1,128)}, u32[]{:S(2)}) copy-start(f32[1,2048]{1,0:T(1,128)} %param.10) | copy-start | bytes 24580
  134.7 14.2 %copy-start.1 = (s32[2048]{0:T(1024)}, s32[2048]{0:T(1024)S(1)}, u32[]{:S(2)}) copy-start(s32[2048]{0:T(1024)S(1)} %convert_reduce_fusion) | copy-start | bytes 24580
  260.7 38.6 %copy-start = (f32[512,2048]{1,0:T(8,128)S(1)}, f32[512,2048]{1,0:T(8,128)}, u32[]{:S(2)}) copy-start(f32[512,2048]{1,0:T(8,128)} %get-tuple-element.19) | copy-start | bytes 12582916
Sparse Core Ops, SparseCore 0:
  50.3 29.0 all-gather.8
  81.0 28.5 all-gather.10
  111.2 28.5 all-gather.12
  141.2 28.5 all-gather.14
